TPU v7x, 256 devices: a whole 4x4x8 slice. The times are simulated.
256 devices in a mesh: row: 8 (over x, core), col: 32 (over y, z).
Axes of the slice: x: 4, y: 4, z: 8, core: 2. Of those that a mesh axis runs over, the one named last changes fastest.
Arguments:
- features: bfloat16 [65536, 256], P(('row', 'col')), may hold values from -6 to 6
- neighbours: int32 [10, 65536], P(None, ('row', 'col')), may hold values from 0 to 511, as said below
- halo_ids: int32 [256, 1, 256], P(('row', 'col')), may hold values from 0 to 255
- w_self: bfloat16 [256, 256], replicated, may hold values from -0.375 to 0.375
- w_neigh: bfloat16 [256, 256], replicated, may hold values from -0.75 to 0.75
- b_sage: float32 [256], replicated, may hold values from -3 to 3
- w_first: bfloat16 [512, 256], replicated, may hold values from -0.25 to 0.25
- b_first: float32 [256], replicated, may hold values from -3 to 3
- w_second: bfloat16 [256], replicated, may hold values from -1.5 to 1.5
- b_second: float32 [1], replicated, may hold values from -3 to 3
- src_owner: int32 [8, 32, 8192, 1], P('row', 'col'), may hold values from 0 to 31; in each aligned block of 8192 rows (0 to 8191, 8192 to 16383, ..., all dimensions but the last counted through in order) at most 320 rows name the same one
- src_local: int32 [8, 32, 8192], P('row', 'col'), may hold values from 0 to 255
- dst_index: int32 [8, 32, 8192], P('row', 'col'), may hold values from 0 to 2047
- labels: int32 [8, 32, 8192], P('row', 'col'), may hold values 0 or 1
Outputs:
- embeds: bfloat16 [65536, 256], P(('row', 'col'))
- logits: float32 [8, 32, 8192], P('row', 'col')
- node_grad: float32 [65536, 256], P(('row', 'col'))
- grad_self: float32 [256, 256], replicated
- grad_neigh: float32 [256, 256], replicated
- grad_bsage: float32 [256], replicated
- grad_first: float32 [32, 512, 256], P('col')
- grad_bfirst: float32 [32, 256], P('col')
- grad_second: float32 [32, 256], P('col')
Inputs may be any that keep to these rules, and one draw needn't show every extreme that they name: `neighbours`: in each partition every one of the 256 received rows (values 256 and up) is named by exactly one entry; the other entries name the partition's own rows. `src_owner`: among the 8192 edges of one tile at most 320 name the same source partition, and that many are reached.
All inputs are finite; a program needn't handle non-finite values. No bound on the sum of `labels` on one device may be relied on, other than what follows from the above.
Results may differ from a plain program's by a relative error of at most 0.0052.
Values may be sent and summed in bfloat16 or wider, within the bound.
No kernel may reach another device: no remote copies, remote signals or barrier semaphores. Data moves between devices by JAX's collectives and lax.ppermute only.
A program may use at most 128 MiB of HBM per device.

v0:
```python
import jax
import jax.numpy as jnp
from jax import lax
from jax.sharding import PartitionSpec as P


def per_device(
    features,
    neighbours,
    halo_ids,
    w_self,
    w_neigh,
    b_sage,
    w_first,
    b_first,
    w_second,
    b_second,
    src_owner,
    src_local,
    dst_index,
    labels,
):
    node_dev, feat_width = features.shape
    fanout = neighbours.shape[0]
    row_count = lax.axis_size("row")
    col_count = lax.axis_size("col")
    outgoing = features[halo_ids[0]]
    halo_count = outgoing.shape[0]
    outgoing = outgoing.reshape(halo_count, row_count, col_count, feat_width)
    received = lax.all_to_all(
        lax.all_to_all(outgoing, "row", split_axis=1, concat_axis=1, tiled=True),
        "col",
        split_axis=2,
        concat_axis=2,
        tiled=True,
    )
    extended = jnp.concatenate([features, received.reshape(-1, feat_width)], axis=0)
    gathered = extended[neighbours].astype(jnp.float32)
    aggregate = (jnp.sum(gathered, axis=0) / fanout).astype(jnp.bfloat16)
    embed_f = jnp.dot(features, w_self, preferred_element_type=jnp.float32)
    embed_f = embed_f + jnp.dot(aggregate, w_neigh, preferred_element_type=jnp.float32) + b_sage
    embeds = embed_f.astype(jnp.bfloat16)
    owners = src_owner[0, 0, :, 0]
    local_rows = src_local[0, 0]
    dest_rows = dst_index[0, 0]
    targets = labels[0, 0].astype(jnp.float32)
    edge_count = owners.shape[0]
    src_block = lax.all_gather(embeds, "col", axis=0, tiled=True)
    block_rows = owners * node_dev + local_rows
    src_embed = src_block[block_rows]
    dst_block = lax.all_gather(embeds, "row", axis=0, tiled=True)
    dst_embed = dst_block[dest_rows]
    w_src = w_first[:feat_width]
    w_dst = w_first[feat_width:]
    preact = jnp.dot(src_embed, w_src, preferred_element_type=jnp.float32)
    preact = preact + jnp.dot(dst_embed, w_dst, preferred_element_type=jnp.float32) + b_first
    gate_sig = jax.nn.sigmoid(preact)
    hidden = preact * gate_sig
    hidden_b = hidden.astype(jnp.bfloat16)
    logits = jnp.dot(hidden_b, w_second, preferred_element_type=jnp.float32) + b_second[0]
    dlogit = jax.nn.sigmoid(logits) - targets
    second_f = w_second.astype(jnp.float32)
    dpreact = dlogit[:, None] * second_f[None, :] * gate_sig * (1.0 + preact * (1.0 - gate_sig))
    dpreact_b = dpreact.astype(jnp.bfloat16)
    part_second = jnp.sum(hidden * dlogit[:, None], axis=0)
    part_bfirst = jnp.sum(dpreact, axis=0)
    grad_src = jnp.dot(src_embed.T, dpreact_b, preferred_element_type=jnp.float32)
    grad_dst = jnp.dot(dst_embed.T, dpreact_b, preferred_element_type=jnp.float32)
    part_first = jnp.concatenate([grad_src, grad_dst], axis=0)
    decoder_sums = lax.psum((part_first, part_bfirst, part_second), "row")
    src_rows_g = jnp.dot(dpreact_b, w_src.T, preferred_element_type=jnp.float32).astype(
        jnp.bfloat16
    )
    dst_rows_g = jnp.dot(dpreact_b, w_dst.T, preferred_element_type=jnp.float32).astype(
        jnp.bfloat16
    )
    src_acc = (
        jnp.zeros((src_block.shape[0], feat_width), jnp.float32)
        .at[block_rows]
        .add(src_rows_g.astype(jnp.float32))
    )
    src_grad = lax.psum_scatter(src_acc, "col", scatter_dimension=0, tiled=True)
    dest_acc = (
        jnp.zeros((dst_block.shape[0], feat_width), jnp.float32)
        .at[dest_rows]
        .add(dst_rows_g.astype(jnp.float32))
    )
    dest_grad = lax.psum_scatter(dest_acc, "row", scatter_dimension=0, tiled=True)
    node_grad = src_grad + dest_grad
    node_grad_b = node_grad.astype(jnp.bfloat16)
    part_self = jnp.dot(features.T, node_grad_b, preferred_element_type=jnp.float32)
    part_neigh = jnp.dot(aggregate.T, node_grad_b, preferred_element_type=jnp.float32)
    part_bsage = jnp.sum(node_grad, axis=0)
    encoder_sums = lax.psum((part_self, part_neigh, part_bsage), ("row", "col"))
    return (
        embeds,
        logits.reshape(1, 1, edge_count),
        node_grad,
        encoder_sums[0],
        encoder_sums[1],
        encoder_sums[2],
        decoder_sums[0][None],
        decoder_sums[1][None],
        decoder_sums[2][None],
    )


def solution(mesh):
    placed = (
        P(("row", "col"), None),
        P(None, ("row", "col")),
        P(("row", "col"), None, None),
        P(),
        P(),
        P(),
        P(),
        P(),
        P(),
        P(),
        P("row", "col", None, None),
        P("row", "col", None),
        P("row", "col", None),
        P("row", "col", None),
    )
    return jax.shard_map(
        per_device,
        mesh=mesh,
        in_specs=placed,
        out_specs=(
            P(("row", "col"), None),
            P("row", "col", None),
            P(("row", "col"), None),
            P(),
            P(),
            P(),
            P("col", None, None),
            P("col", None),
            P("col", None),
        ),
        check_vma=False,
    )
```

profile of v0, /device:TPU:8, one launch (start us, length us, event | category | flops | bytes accessed | tf_op | source)
XLA Modules:
  0.0 875.0 jit_solution(14454785513505962907)
XLA Ops:
  8.0 2.5 gather_fusion
  10.5 4.4 all-to-all-start
  15.7 5.4 all-to-all-done
  21.8 11.7 %all-to-all-start.1 = ((bf16[1,8,32,256]{3,1,0,2:T(8,128)(2,1)}), bf16[1,8,32,256]{3,1,0,2:T(8,128)(2,1)S(1)}, u32[]{:S(2)}, u32[]{:S(2)}) async-start(bf16[1,8,32,256]{3,1,0,2:T(8,128)(2,1)} %copy.26), calls=%async_computation.1 | async-start | bytes 262144 | tf_op jit(solution)/shard_map/all_to_all | solution.py:30
  33.6 1.1 fusion.26
  34.7 7.9 all-to-all-done.1
  43.6 7.6 gather_fusion.1
  54.1 18.4 %all-gather.5.cloned.1.call-done = bf16[2048,256]{1,0:T(8,128)(2,1)} async-done(((bf16[256,256]{1,0:T(8,128)(2,1)}), bf16[2048,256]{1,0:T(8,128)(2,1)}) %all-gather.5.cloned.1.call-update) | async-done | bytes 1048592 | tf_op jit(solution)/shard_map/all_gather | solution.py:51
  72.6 32.2 %gather_fusion.3 = bf16[8192,256]{1,0:T(8,128)(2,1)} fusion(bf16[2048,256]{1,0:T(8,128)(2,1)} %all-gather.5.cloned.1.call-done, s32[8192]{0:T(1024)S(1)} %broadcast_clamp_fusion), kind=kCustom, calls=%fused_computation.3 | custom fusion | bytes 8421376 | tf_op jit(solution)/shard_map/gather | solution.py:52
  104.8 51.4 %all-gather.3.cloned.1.call-done = bf16[8192,256]{1,0:T(8,128)(2,1)} async-done(((bf16[256,256]{1,0:T(8,128)(2,1)}), bf16[8192,256]{1,0:T(8,128)(2,1)}) %all-gather.3.cloned.1.call-update) | async-done | bytes 4194320 | tf_op jit(solution)/shard_map/all_gather | solution.py:48
  156.2 33.6 %gather_fusion.2 = bf16[8192,256]{1,0:T(8,128)(2,1)} fusion(bf16[8192,256]{1,0:T(8,128)(2,1)} %all-gather.3.cloned.1.call-done, s32[8192]{0:T(1024)S(1)} %broadcast_clamp_fusion.1), kind=kCustom, calls=%fused_computation.2 | custom fusion | bytes 8421376 | tf_op jit(solution)/shard_map/gather | solution.py:50
  189.8 3.6 fusion.16
  193.4 1.3 fusion
  194.7 2.4 fusion.6
  197.8 5.9 fusion.24
  203.6 2.0 copy-done.2
  205.6 4.5 fusion.1
  210.1 46.0 %scatter_custom_fusion.1 = f32[2048,256]{1,0:T(8,128)} fusion(s32[8192]{0:T(1024)S(1)} %bitcast.48, f32[8192,256]{1,0:T(8,128)} %fusion.1, f32[]{:T(128)} %constant.11.clone.1), kind=kCustom, calls=%fused_computation.25 | custom fusion | flops 2097152 | bytes 2097664 | tf_op jit(solution)/shard_map/scatter-add | solution.py:86
  256.4 6.7 fusion.2
  263.1 48.3 %scatter_custom_fusion = f32[8192,256]{1,0:T(8,128)} fusion(s32[8192]{0:T(1024)S(1)} %bitcast.46, f32[8192,256]{1,0:T(8,128)} %fusion.2, f32[]{:T(128)} %constant.11.clone.1), kind=kCustom, calls=%fused_computation.16 | custom fusion | flops 2097152 | bytes 8389120 | tf_op jit(solution)/shard_map/scatter-add | solution.py:80
  311.5 4.8 fusion.27
  316.3 221.9 %reduce-scatter.3.cloned.1.call-done = f32[256,256]{1,0:T(8,128)} async-done(((f32[8192,256]{1,0:T(8,128)}), f32[256,256]{1,0:T(8,128)}) %reduce-scatter.3.cloned.1.call-update) | async-done | bytes 262160 | tf_op jit(solution)/shard_map/reduce_scatter | solution.py:82
  538.3 1.1 fusion.25
  539.4 0.9 fusion.18
  541.3 4.8 fusion.28
  547.0 13.0 %all-reduce.1 = (f32[1,256]{1,0:T(1,128)}, f32[1,256]{1,0:T(1,128)}) all-reduce(f32[1,256]{1,0:T(1,128)S(1)} %bitcast.52, f32[1,256]{1,0:T(1,128)S(1)} %bitcast.53), channel_id=1, replica_groups=mesh['row'=8,'col'=32] {'row'}, use_global_device_ids=true, to_apply=%region_11.0 | all-reduce | flops 512 | bytes 4096 | tf_op jit(solution)/shard_map/psum | solution.py:70
  560.0 74.7 %psum.44 = f32[256]{0:T(256)} all-reduce(f32[256]{0:T(256)S(1)} %get-tuple-element.42), channel_id=1, replica_groups=mesh['row'=8,'col'=32] {'row','col'}, use_global_device_ids=true, to_apply=%region_8.0 | all-reduce | flops 256 | bytes 2048 | tf_op jit(solution)/shard_map/psum | solution.py:94
  634.6 162.6 %all-reduce.7.cloned.1.call-done = (f32[256,256]{0,1:T(8,128)}, f32[256,256]{1,0:T(8,128)}) async-done(((f32[256,256]{0,1:T(8,128)}, f32[256,256]{1,0:T(8,128)}), (f32[256,256]{0,1:T(8,128)}, f32[256,256]{1,0:T(8,128)})) %all-reduce.7.cloned.1.call-update) | async-done | bytes 524304 | tf_op jit(solution)/shard_map/psum | solution.py:94
  797.2 1.8 copy.28
  799.0 65.6 %all-reduce.5.cloned.1.call-done = f32[1,512,256]{2,1,0:T(8,128)} async-done(((f32[1,512,256]{2,1,0:T(8,128)}), f32[1,512,256]{2,1,0:T(8,128)}) %all-reduce.5.cloned.1.call-update) | async-done | bytes 524304 | tf_op jit(solution)/shard_map/psum | solution.py:70
  864.6 1.7 copy.33
  866.2 1.9 copy.34
  (62 shorter events, 8.2 us)
Async XLA Ops:
  7.2 26.4 %copy-start = (bf16[256,256]{1,0:T(8,128)(2,1)S(1)}, bf16[256,256]{1,0:T(8,128)(2,1)}, u32[]{:S(2)}) copy-start(bf16[256,256]{1,0:T(8,128)(2,1)} %param.17) | copy-start | bytes 393220
  7.2 44.2 %copy-start.13 = (f32[256]{0:T(256)S(1)}, f32[256]{0:T(256)}, u32[]{:S(2)}) copy-start(f32[256]{0:T(256)} %param.19) | copy-start | bytes 3076
  7.2 44.2 %copy-start.7 = (bf16[256,256]{1,0:T(8,128)(2,1)S(1)}, bf16[256,256]{1,0:T(8,128)(2,1)}, u32[]{:S(2)}) copy-start(bf16[256,256]{1,0:T(8,128)(2,1)} %param.18) | copy-start | bytes 393220
  10.5 42.7 %copy-start.14 = (bf16[256]{0:T(256)(128)(2,1)S(1)}, bf16[256]{0:T(256)(128)(2,1)}, u32[]{:S(2)}) copy-start(bf16[256]{0:T(256)(128)(2,1)} %param.22) | copy-start | bytes 1540
  10.5 43.4 %copy-start.10 = (s32[1,1,8192]{2,1,0:T(1,128)S(1)}, s32[1,1,8192]{2,1,0:T(1,128)}, u32[]{:S(2)}) copy-start(s32[1,1,8192]{2,1,0:T(1,128)} %param.27) | copy-start | bytes 98308
  10.5 43.4 %copy-start.8 = (s32[1,1,8192]{2,1,0:T(1,128)S(1)}, s32[1,1,8192]{2,1,0:T(1,128)}, u32[]{:S(2)}) copy-start(s32[1,1,8192]{2,1,0:T(1,128)} %param.25) | copy-start | bytes 98308
  10.5 43.5 %copy-start.9 = (s32[1,1,8192,1]{2,3,1,0:T(1,128)S(1)}, s32[1,1,8192,1]{2,3,1,0:T(1,128)}, u32[]{:S(2)}) copy-start(s32[1,1,8192,1]{2,3,1,0:T(1,128)} %param.24) | copy-start | bytes 98308
  10.5 43.5 %copy-start.11 = (s32[1,1,8192]{2,1,0:T(1,128)S(1)}, s32[1,1,8192]{2,1,0:T(1,128)}, u32[]{:S(2)}) copy-start(s32[1,1,8192]{2,1,0:T(1,128)} %param.26) | copy-start | bytes 98308
  10.5 10.6 %all-to-all-start = ((bf16[1,8,32,256]{3,2,0,1:T(8,128)(2,1)}), bf16[1,8,32,256]{3,2,0,1:T(8,128)(2,1)S(1)}, u32[]{:S(2)}, u32[]{:S(2)}) async-start(bf16[1,8,32,256]{3,2,0,1:T(8,128)(2,1)} %bitcast.3), calls=%async_computation | async-start | bytes 262144 | tf_op jit(solution)/shard_map/all_to_all | solution.py:31
  21.8 20.8 %all-to-all-start.1 = ((bf16[1,8,32,256]{3,1,0,2:T(8,128)(2,1)}), bf16[1,8,32,256]{3,1,0,2:T(8,128)(2,1)S(1)}, u32[]{:S(2)}, u32[]{:S(2)}) async-start(bf16[1,8,32,256]{3,1,0,2:T(8,128)(2,1)} %copy.26), calls=%async_computation.1 | async-start | bytes 262144 | tf_op jit(solution)/shard_map/all_to_all | solution.py:30
  33.6 39.0 %all-gather.5.cloned.1.call-start = ((), (), s32[]{:S(2)}) async-start(), calls=%async_computation.5 | async-start | bytes 1179648 | tf_op jit(solution)/shard_map/all_gather | solution.py:51
  52.3 103.9 %all-gather.3.cloned.1.call-start = ((), (), s32[]{:S(2)}) async-start(), calls=%async_computation.4 | async-start | bytes 4325376 | tf_op jit(solution)/shard_map/all_gather | solution.py:48
  53.0 263.3 %reduce-scatter.5.cloned.1.call-start = ((), (), s32[]{:S(2)}) async-start(), calls=%async_computation.7 | async-start | bytes 2359296 | tf_op jit(solution)/shard_map/reduce_scatter | solution.py:88
  104.8 85.0 %copy-start.6 = (bf16[512,256]{1,0:T(8,128)(2,1)S(1)}, bf16[512,256]{1,0:T(8,128)(2,1)}, u32[]{:S(2)}) copy-start(bf16[512,256]{1,0:T(8,128)(2,1)} %param.20) | copy-start | bytes 786436
  189.8 3.6 copy-start.3
  189.8 3.6 copy-start.12
  203.6 2.0 copy-start.2
  256.2 282.1 %reduce-scatter.3.cloned.1.call-start = ((), (), s32[]{:S(2)}) async-start(), calls=%async_computation.6 | async-start | bytes 8650752 | tf_op jit(solution)/shard_map/reduce_scatter | solution.py:82
  311.5 228.8 %copy-start.4 = (bf16[256,256]{1,0:T(8,128)(2,1)S(1)}, bf16[256,256]{1,0:T(8,128)(2,1)}, u32[]{:S(2)}) copy-start(bf16[256,256]{1,0:T(8,128)(2,1)} %param.14) | copy-start | bytes 393220
  311.5 485.7 %all-reduce.7.cloned.1.call-start = ((), (), s32[]{:S(2)}) async-start(), calls=%async_computation.9 | async-start | bytes 1048576 | tf_op jit(solution)/shard_map/psum | solution.py:94
  539.4 6.7 copy-start.5
  541.3 326.8 %copy-start.1 = (bf16[256,256]{1,0:T(8,128)(2,1)S(1)}, bf16[256,256]{1,0:T(8,128)(2,1)}, u32[]{:S(2)}) copy-start(bf16[256,256]{1,0:T(8,128)(2,1)} %param.17) | copy-start | bytes 393220
  541.3 323.3 %all-reduce.5.cloned.1.call-start = ((), (), s32[]{:S(2)}) async-start(), calls=%async_computation.8 | async-start | bytes 1048576 | tf_op jit(solution)/shard_map/psum | solution.py:70
Sparse Core Ops, SparseCore 0:
  52.4 20.1 all-gather.4
  75.7 80.4 all-gather.2
  256.3 34.6 reduce-scatter.4
  311.6 226.6 reduce-scatter.2
  545.3 251.9 all-reduce.6
  800.1 64.4 all-reduce.4
where the time goes:
time: 876 us; the launch traced here: 875 us
  waiting for transfers between devices  534 us (61%)
  other arithmetic  105 us (12%)
  blocking collectives  87.7 us (10%)
  local copies, waits for them, and re-layouts  84.1 us (10%)
  matrix products  31.8 us (4%)
  starting transfers between devices  16.8 us (2%)
  between operations  15.1 us (2%)
    reduce_scatter x1, waiting for transfers between devices, per_device(): src_grad = lax.psum_scatter(src_acc, 'col', scatter_dimension=0, tiled=True)  222 us
    psum x1, waiting for transfers between devices, per_device(): encoder_sums = lax.psum((part_self, part_neigh, part_bsage), ('row', 'col'))  163 us
    psum x1, blocking collectives, per_device(): encoder_sums = lax.psum((part_self, part_neigh, part_bsage), ('row', 'col'))  74.7 us
    psum x1, waiting for transfers between devices, per_device(): decoder_sums = lax.psum((part_first, part_bfirst, part_second), 'row')  65.6 us
    all_gather x1, waiting for transfers between devices, per_device(): src_block = lax.all_gather(embeds, 'col', axis=0, tiled=True)  51.4 us
    scatter-add x1, other arithmetic, per_device(): src_acc = jnp.zeros((src_block.shape[0], feat_width), jnp.float32).at[blo...  48.3 us
    scatter-add x1, other arithmetic, per_device(): dest_acc = jnp.zeros((dst_block.shape[0], feat_width), jnp.float32).at[de...  46 us
    gather x1, local copies, waits for them, and re-layouts, per_device(): src_embed = src_block[block_rows]  33.6 us
  transfers between devices with their start and end apart: 8, of which 7 were waited for; matrix products, arithmetic and copies ran while one was open for 12% of the time, Pallas kernels for 0%

commit v1 on v0

--- a/solution.py
+++ b/solution.py
@@ -91,7 +91,9 @@
     part_self = jnp.dot(features.T, node_grad_b, preferred_element_type=jnp.float32)
     part_neigh = jnp.dot(aggregate.T, node_grad_b, preferred_element_type=jnp.float32)
     part_bsage = jnp.sum(node_grad, axis=0)
-    encoder_sums = lax.psum((part_self, part_neigh, part_bsage), ("row", "col"))
+    encoder_sums = jax.lax.psum(
+        jax.lax.psum((part_self, part_neigh, part_bsage), axis_name="col"), axis_name="row"
+    )
     return (
         embeds,
         logits.reshape(1, 1, edge_count),

time: 876 us -> 789 us (0.901); the launches traced: 875 us -> 776 us
  waiting for transfers between devices: 534 us -> 447 us
  blocking collectives: 87.7 us -> 75.8 us
    psum x2, waiting for transfers between devices: 228 us -> 141 us  [the longest x1 141 us: per_device(): jax.lax.psum((part_self, part_neigh, part_bsage), axis_name='col')]
    psum x2, blocking collectives: 87.7 us -> 75.8 us  [the longest x1 62.9 us: per_device(): jax.lax.psum((part_self, part_neigh, part_bsage), axis_name='col')]
  transfers between devices with their start and end apart: 8 -> 8, of which waited for: 7 -> 6; matrix products, arithmetic and copies ran while one was open for 12% -> 13% of each run, Pallas kernels for 0% -> 0%
where the time goes in v1:
time: 789 us; the launch traced here: 776 us
  waiting for transfers between devices  447 us (57%)
  other arithmetic  105 us (13%)
  local copies, waits for them, and re-layouts  84.2 us (11%)
  blocking collectives  75.8 us (10%)
  matrix products  31.8 us (4%)
  starting transfers between devices  16.8 us (2%)
  between operations  15.1 us (2%)
    reduce_scatter x1, waiting for transfers between devices, per_device(): src_grad = lax.psum_scatter(src_acc, 'col', scatter_dimension=0, tiled=True)  222 us
    psum x1, waiting for transfers between devices, per_device(): jax.lax.psum((part_self, part_neigh, part_bsage), axis_name='col')  141 us
    psum x1, blocking collectives, per_device(): jax.lax.psum((part_self, part_neigh, part_bsage), axis_name='col')  62.9 us
    all_gather x1, waiting for transfers between devices, per_device(): src_block = lax.all_gather(embeds, 'col', axis=0, tiled=True)  51.3 us
    scatter-add x1, other arithmetic, per_device(): src_acc = jnp.zeros((src_block.shape[0], feat_width), jnp.float32).at[blo...  48.3 us
    scatter-add x1, other arithmetic, per_device(): dest_acc = jnp.zeros((dst_block.shape[0], feat_width), jnp.float32).at[de...  46 us
    gather x1, local copies, waits for them, and re-layouts, per_device(): src_embed = src_block[block_rows]  33.7 us
    gather x1, local copies, waits for them, and re-layouts, per_device(): dst_embed = dst_block[dest_rows]  32.3 us
  transfers between devices with their start and end apart: 8, of which 6 were waited for; matrix products, arithmetic and copies ran while one was open for 13% of the time, Pallas kernels for 0%

profile of v1, /device:TPU:8, one launch (start us, length us, event | category | flops | bytes accessed | tf_op | source)
XLA Modules:
  0.0 776.3 jit_solution(7574049874547176835)
XLA Ops:
  8.0 2.5 gather_fusion
  10.5 4.4 all-to-all-start
  15.7 5.4 all-to-all-done
  21.8 11.7 %all-to-all-start.1 = ((bf16[1,8,32,256]{3,1,0,2:T(8,128)(2,1)}), bf16[1,8,32,256]{3,1,0,2:T(8,128)(2,1)S(1)}, u32[]{:S(2)}, u32[]{:S(2)}) async-start(bf16[1,8,32,256]{3,1,0,2:T(8,128)(2,1)} %copy.26), calls=%async_computation.1 | async-start | bytes 262144 | tf_op jit(solution)/shard_map/all_to_all | solution.py:30
  33.6 1.1 fusion.26
  34.7 7.9 %all-to-all-done.1 = bf16[1,8,32,256]{3,1,0,2:T(8,128)(2,1)S(1)} async-done(((bf16[1,8,32,256]{3,1,0,2:T(8,128)(2,1)}), bf16[1,8,32,256]{3,1,0,2:T(8,128)(2,1)S(1)}, u32[]{:S(2)}, u32[]{:S(2)}) %all-to-all-start.1) | async-done | bytes 131104 | tf_op jit(solution)/shard_map/all_to_all | solution.py:30
  43.6 7.6 gather_fusion.1
  54.1 18.4 %all-gather.5.cloned.1.call-done = bf16[2048,256]{1,0:T(8,128)(2,1)} async-done(((bf16[256,256]{1,0:T(8,128)(2,1)}), bf16[2048,256]{1,0:T(8,128)(2,1)}) %all-gather.5.cloned.1.call-update) | async-done | bytes 1048592 | tf_op jit(solution)/shard_map/all_gather | solution.py:51
  72.6 32.3 %gather_fusion.3 = bf16[8192,256]{1,0:T(8,128)(2,1)} fusion(bf16[2048,256]{1,0:T(8,128)(2,1)} %all-gather.5.cloned.1.call-done, s32[8192]{0:T(1024)S(1)} %broadcast_clamp_fusion), kind=kCustom, calls=%fused_computation.3 | custom fusion | bytes 8421376 | tf_op jit(solution)/shard_map/gather | solution.py:52
  104.9 51.3 %all-gather.3.cloned.1.call-done = bf16[8192,256]{1,0:T(8,128)(2,1)} async-done(((bf16[256,256]{1,0:T(8,128)(2,1)}), bf16[8192,256]{1,0:T(8,128)(2,1)}) %all-gather.3.cloned.1.call-update) | async-done | bytes 4194320 | tf_op jit(solution)/shard_map/all_gather | solution.py:48
  156.2 33.7 %gather_fusion.2 = bf16[8192,256]{1,0:T(8,128)(2,1)} fusion(bf16[8192,256]{1,0:T(8,128)(2,1)} %all-gather.3.cloned.1.call-done, s32[8192]{0:T(1024)S(1)} %broadcast_clamp_fusion.1), kind=kCustom, calls=%fused_computation.2 | custom fusion | bytes 8421376 | tf_op jit(solution)/shard_map/gather | solution.py:50
  189.9 3.6 fusion.16
  193.5 1.3 fusion
  194.7 2.4 fusion.6
  197.8 5.9 fusion.24
  203.7 2.0 copy-done.2
  205.7 4.5 fusion.1
  210.2 46.0 %scatter_custom_fusion.1 = f32[2048,256]{1,0:T(8,128)} fusion(s32[8192]{0:T(1024)S(1)} %bitcast.48, f32[8192,256]{1,0:T(8,128)} %fusion.1, f32[]{:T(128)} %constant.11.clone.1), kind=kCustom, calls=%fused_computation.25 | custom fusion | flops 2097152 | bytes 2097664 | tf_op jit(solution)/shard_map/scatter-add | solution.py:86
  256.5 6.7 fusion.2
  263.2 48.3 %scatter_custom_fusion = f32[8192,256]{1,0:T(8,128)} fusion(s32[8192]{0:T(1024)S(1)} %bitcast.46, f32[8192,256]{1,0:T(8,128)} %fusion.2, f32[]{:T(128)} %constant.11.clone.1), kind=kCustom, calls=%fused_computation.16 | custom fusion | flops 2097152 | bytes 8389120 | tf_op jit(solution)/shard_map/scatter-add | solution.py:80
  311.6 4.8 fusion.27
  316.4 222.1 %reduce-scatter.3.cloned.1.call-done = f32[256,256]{1,0:T(8,128)} async-done(((f32[8192,256]{1,0:T(8,128)}), f32[256,256]{1,0:T(8,128)}) %reduce-scatter.3.cloned.1.call-update) | async-done | bytes 262160 | tf_op jit(solution)/shard_map/reduce_scatter | solution.py:82
  538.5 1.1 fusion.25
  539.6 0.9 fusion.18
  540.6 0.9 convolution_bitcast_fusion
  541.6 4.8 fusion.28
  547.2 141.1 %all-reduce.6.cloned.1.call-done = (f32[256,256]{0,1:T(8,128)}, f32[256,256]{1,0:T(8,128)}) async-done(((f32[256,256]{0,1:T(8,128)}, f32[256,256]{1,0:T(8,128)}), (f32[256,256]{0,1:T(8,128)}, f32[256,256]{1,0:T(8,128)})) %all-reduce.6.cloned.1.call-update) | async-done | bytes 524304 | tf_op jit(solution)/shard_map/psum | solution.py:95
  688.3 62.9 %psum.67 = f32[256]{0:T(256)S(1)} all-reduce(f32[256]{0:T(256)S(1)} %get-tuple-element.46), channel_id=1, replica_groups=mesh['row'=8,'col'=32] {'col'}, use_global_device_ids=true, to_apply=%region_10.0 | all-reduce | flops 256 | bytes 2048 | tf_op jit(solution)/shard_map/psum | solution.py:95
  751.2 13.0 %all-reduce.1 = (f32[256]{0:T(256)}, f32[1,256]{1,0:T(1,128)}, f32[1,256]{1,0:T(1,128)}) all-reduce(f32[256]{0:T(256)S(1)} %psum.67, f32[1,256]{1,0:T(1,128)S(1)} %bitcast.52, f32[1,256]{1,0:T(1,128)S(1)} %bitcast.53), channel_id=1, replica_groups=mesh['row'=8,'col'=32] {'row'}, use_global_device_ids=true, to_apply=%region_11.0 | all-reduce | flops 768 | bytes 6144 | tf_op jit(solution)/shard_map/psum | solution.py:94
  764.1 1.8 copy.28
  765.9 1.7 copy.35
  767.6 1.9 copy.36
  (62 shorter events, 7.3 us)
Async XLA Ops:
  7.2 26.4 %copy-start = (bf16[256,256]{1,0:T(8,128)(2,1)S(1)}, bf16[256,256]{1,0:T(8,128)(2,1)}, u32[]{:S(2)}) copy-start(bf16[256,256]{1,0:T(8,128)(2,1)} %param.17) | copy-start | bytes 393220
  7.2 44.2 %copy-start.13 = (f32[256]{0:T(256)S(1)}, f32[256]{0:T(256)}, u32[]{:S(2)}) copy-start(f32[256]{0:T(256)} %param.19) | copy-start | bytes 3076
  7.2 44.2 %copy-start.7 = (bf16[256,256]{1,0:T(8,128)(2,1)S(1)}, bf16[256,256]{1,0:T(8,128)(2,1)}, u32[]{:S(2)}) copy-start(bf16[256,256]{1,0:T(8,128)(2,1)} %param.18) | copy-start | bytes 393220
  10.5 42.7 %copy-start.14 = (bf16[256]{0:T(256)(128)(2,1)S(1)}, bf16[256]{0:T(256)(128)(2,1)}, u32[]{:S(2)}) copy-start(bf16[256]{0:T(256)(128)(2,1)} %param.22) | copy-start | bytes 1540
  10.5 43.4 %copy-start.10 = (s32[1,1,8192]{2,1,0:T(1,128)S(1)}, s32[1,1,8192]{2,1,0:T(1,128)}, u32[]{:S(2)}) copy-start(s32[1,1,8192]{2,1,0:T(1,128)} %param.27) | copy-start | bytes 98308
  10.5 43.4 %copy-start.8 = (s32[1,1,8192]{2,1,0:T(1,128)S(1)}, s32[1,1,8192]{2,1,0:T(1,128)}, u32[]{:S(2)}) copy-start(s32[1,1,8192]{2,1,0:T(1,128)} %param.25) | copy-start | bytes 98308
  10.5 43.5 %copy-start.9 = (s32[1,1,8192,1]{2,3,1,0:T(1,128)S(1)}, s32[1,1,8192,1]{2,3,1,0:T(1,128)}, u32[]{:S(2)}) copy-start(s32[1,1,8192,1]{2,3,1,0:T(1,128)} %param.24) | copy-start | bytes 98308
  10.5 43.5 %copy-start.11 = (s32[1,1,8192]{2,1,0:T(1,128)S(1)}, s32[1,1,8192]{2,1,0:T(1,128)}, u32[]{:S(2)}) copy-start(s32[1,1,8192]{2,1,0:T(1,128)} %param.26) | copy-start | bytes 98308
  10.5 10.6 %all-to-all-start = ((bf16[1,8,32,256]{3,2,0,1:T(8,128)(2,1)}), bf16[1,8,32,256]{3,2,0,1:T(8,128)(2,1)S(1)}, u32[]{:S(2)}, u32[]{:S(2)}) async-start(bf16[1,8,32,256]{3,2,0,1:T(8,128)(2,1)} %bitcast.3), calls=%async_computation | async-start | bytes 262144 | tf_op jit(solution)/shard_map/all_to_all | solution.py:31
  21.8 20.8 %all-to-all-start.1 = ((bf16[1,8,32,256]{3,1,0,2:T(8,128)(2,1)}), bf16[1,8,32,256]{3,1,0,2:T(8,128)(2,1)S(1)}, u32[]{:S(2)}, u32[]{:S(2)}) async-start(bf16[1,8,32,256]{3,1,0,2:T(8,128)(2,1)} %copy.26), calls=%async_computation.1 | async-start | bytes 262144 | tf_op jit(solution)/shard_map/all_to_all | solution.py:30
  33.6 39.0 %all-gather.5.cloned.1.call-start = ((), (), s32[]{:S(2)}) async-start(), calls=%async_computation.5 | async-start | bytes 1179648 | tf_op jit(solution)/shard_map/all_gather | solution.py:51
  52.3 103.9 %all-gather.3.cloned.1.call-start = ((), (), s32[]{:S(2)}) async-start(), calls=%async_computation.4 | async-start | bytes 4325376 | tf_op jit(solution)/shard_map/all_gather | solution.py:48
  53.0 263.4 %reduce-scatter.5.cloned.1.call-start = ((), (), s32[]{:S(2)}) async-start(), calls=%async_computation.7 | async-start | bytes 2359296 | tf_op jit(solution)/shard_map/reduce_scatter | solution.py:88
  104.9 85.0 %copy-start.6 = (bf16[512,256]{1,0:T(8,128)(2,1)S(1)}, bf16[512,256]{1,0:T(8,128)(2,1)}, u32[]{:S(2)}) copy-start(bf16[512,256]{1,0:T(8,128)(2,1)} %param.20) | copy-start | bytes 786436
  189.9 3.6 copy-start.3
  189.9 3.6 copy-start.12
  203.7 2.0 copy-start.2
  256.2 282.3 %reduce-scatter.3.cloned.1.call-start = ((), (), s32[]{:S(2)}) async-start(), calls=%async_computation.6 | async-start | bytes 8650752 | tf_op jit(solution)/shard_map/reduce_scatter | solution.py:82
  311.5 229.0 %copy-start.4 = (bf16[256,256]{1,0:T(8,128)(2,1)S(1)}, bf16[256,256]{1,0:T(8,128)(2,1)}, u32[]{:S(2)}) copy-start(bf16[256,256]{1,0:T(8,128)(2,1)} %param.14) | copy-start | bytes 393220
  311.5 376.7 %all-reduce.6.cloned.1.call-start = ((), (), s32[]{:S(2)}) async-start(), calls=%async_computation.8 | async-start | bytes 1048576 | tf_op jit(solution)/shard_map/psum | solution.py:95
  539.6 6.7 copy-start.5
  541.5 227.9 %copy-start.1 = (bf16[256,256]{1,0:T(8,128)(2,1)S(1)}, bf16[256,256]{1,0:T(8,128)(2,1)}, u32[]{:S(2)}) copy-start(bf16[256,256]{1,0:T(8,128)(2,1)} %param.17) | copy-start | bytes 393220
  541.5 222.6 %all-reduce.8.cloned.1.call-start = ((), (), s32[]{:S(2)}) async-start(), calls=%async_computation.9 | async-start | bytes 2097152 | tf_op jit(solution)/shard_map/psum | solution.py:94
Sparse Core Ops, SparseCore 0:
  52.4 20.1 all-gather.4
  75.7 80.4 all-gather.2
  256.3 34.6 reduce-scatter.4
  311.6 226.8 reduce-scatter.2
  542.8 145.4 all-reduce.5
  691.2 65.9 all-reduce.7
